TPU v7x, 32 devices: a whole 2x2x4 slice. The times are simulated.
32 devices in a mesh: group: 2 (over x), env: 16 (over z, y, core).
Axes of the slice: x: 2, y: 2, z: 4, core: 2. Of those that a mesh axis runs over, the one named last changes fastest.
Arguments:
- descriptors: bfloat16 [16384, 1024], P(('group', 'env')), parts along dimension 0, may hold values from 0 to 32
- sparse_points: bfloat16 [25600, 1024], P(('group', 'env')), parts along dimension 0, may hold values from 0 to 32
- counts: int32 [32, 12], P(('group', 'env')), parts along dimension 0, may hold values from 1 to 128, 512 in all within a row
- energies: float32 [384], P(('group', 'env')), parts along dimension 0, may hold values from -0.75 to 0.75
Outputs:
- design: bfloat16 [384, 12800], P('group', 'env'), parts along dimension 0
- normal_rhs: float32 [25600], P(('group', 'env')), parts along dimension 0
There are 2 independent parts, one for each index of `group`. A program takes and returns all parts, laid end to end along the dimension named above; each array names one. Nothing has to cross between parts.
All inputs are finite; a program needn't handle non-finite values.
Results may differ from a plain program's by a relative error of at most 0.0031.
Values may be sent and summed in bfloat16 or wider, within the bound.
A program may use at most 128 MiB of HBM per device.

v0:
```python
import jax
import jax.numpy as jnp
from jax import lax
from jax.sharding import PartitionSpec as P

EPS = 1e-06


def inverse_norms(values):
    values_f = values.astype(jnp.float32)
    return lax.rsqrt(jnp.sum(values_f * values_f, axis=1) + EPS)


def kernel_block(atom_rows, inv_atoms, sparse_rows, inv_sparse):
    products = lax.dot_general(
        atom_rows, sparse_rows, (((1,), (1,)), ((), ())), preferred_element_type=jnp.float32
    )
    cosine = products * inv_atoms[:, None] * inv_sparse[None, :]
    squared = cosine * cosine
    return squared * squared


def on_device(descriptors, sparse_points, counts, energies):
    atoms_here = descriptors.shape[0]
    all_energies = lax.all_gather(energies, "env", axis=0, tiled=True)
    inv_atoms = inverse_norms(descriptors)
    seg_ends = jnp.cumsum(counts[0])
    seg_starts = seg_ends - counts[0]
    positions = jnp.arange(atoms_here, dtype=jnp.int32)
    onehot = (
        (positions[None, :] >= seg_starts[:, None]) & (positions[None, :] < seg_ends[:, None])
    ).astype(jnp.float32)
    block_rows = lax.all_gather(sparse_points, "env", axis=0, tiled=True)
    inv_sparse = inverse_norms(block_rows)
    kernel = kernel_block(descriptors, inv_atoms, block_rows, inv_sparse)
    config_part = jnp.dot(onehot, kernel, precision=lax.Precision.HIGHEST)
    design = lax.all_to_all(
        config_part.astype(jnp.bfloat16), "env", split_axis=1, concat_axis=0, tiled=True
    )
    normal_rhs = jnp.dot(all_energies, design.astype(jnp.float32), precision=lax.Precision.HIGHEST)
    return (design, normal_rhs)


def solution(mesh):
    return jax.shard_map(
        on_device,
        mesh=mesh,
        in_specs=(
            P(("group", "env"), None),
            P(("group", "env"), None),
            P(("group", "env"), None),
            P(("group", "env")),
        ),
        out_specs=(P("group", "env"), P(("group", "env"))),
        check_vma=False,
    )
```

profile of v0, /device:TPU:0, one launch (start us, length us, event | category | flops | bytes accessed | tf_op | source)
XLA Modules:
  0.0 245.8 jit_solution(6734748527836936999)
XLA Ops:
  7.2 0.0 copy-start.1
  7.2 0.0 all-gather.2.cloned.1.call-start
  7.2 0.7 all-gather.2.cloned.1.call-update
  7.9 0.8 reduce-window.7
  8.7 1.5 multiply_reduce_fusion.1
  10.2 0.7 bitcast_subtract_fusion
  10.9 135.0 %all-gather.2.cloned.1.call-done = bf16[12800,1024]{1,0:T(8,128)(2,1)} async-done(((bf16[800,1024]{1,0:T(8,128)(2,1)}), bf16[12800,1024]{1,0:T(8,128)(2,1)}) %all-gather.2.cloned.1.call-update) | async-done | bytes 26214416 | tf_op jit(solution)/shard_map/all_gather | solution.py:33
  145.9 9.9 %multiply_reduce_fusion = f32[12800]{0:T(1024)S(1)} fusion(bf16[12800,1024]{1,0:T(8,128)(2,1)} %all-gather.2.cloned.1.call-done), kind=kLoop, calls=%fused_computation | loop fusion | flops 39308800 | bytes 26265600 | tf_op jit(solution)/shard_map/reduce_sum | solution.py:11
  155.8 0.0 copy-done.1
  155.8 25.0 %fusion.14 = f32[512,12800]{1,0:T(8,128)} fusion(bf16[512,1024]{1,0:T(8,128)(2,1)S(1)} %copy-done.1, bf16[12800,1024]{1,0:T(8,128)(2,1)} %all-gather.2.cloned.1.call-done), kind=kOutput, calls=%fused_computation.19 | convolution fusion | flops 13421772800 | bytes 53477376 | tf_op jit(solution)/shard_map/dot_general | solution.py:15
  180.7 15.3 %fusion.5 = bf16[12,12800]{1,0:T(8,128)(2,1)S(1)} fusion(f32[512,12800]{1,0:T(8,128)} %fusion.14, f32[12800]{0:T(1024)S(1)} %add_rsqrt_fusion, f32[512]{0:T(512)S(1)} %add_rsqrt_fusion.1, s32[12]{0:T(128)S(1)} %bitcast.15, s32[12]{0:T(128)S(1)} %bitcast_subtract_fusion), kind=kOutput, calls=%fused_computation.6 | convolution fusion | flops 970104832 | bytes 26574944 | tf_op jit(solution)/shard_map/dot_general | solution.py:36
  196.1 0.5 all_to_all.14
  196.6 0.8 copy.7
  197.5 4.7 %all-to-all-start = ((bf16[12,16,800]{2,0,1:T(8,128)(2,1)}), bf16[12,16,800]{2,0,1:T(8,128)(2,1)S(1)}, u32[]{:S(2)}, u32[]{:S(2)}) async-start(bf16[12,16,800]{2,0,1:T(8,128)(2,1)} %copy.7), calls=%async_computation | async-start | bytes 917504 | tf_op jit(solution)/shard_map/all_to_all | solution.py:37
  202.2 0.0 copy-done.3
  202.2 0.6 dynamic-slice
  203.4 0.0 copy-done.2
  203.4 0.2 dynamic-update-slice
  203.7 34.2 %all-reduce = f32[192]{0:T(256)S(1)} all-reduce(f32[192]{0:T(256)S(1)} %dynamic-update-slice), channel_id=1, replica_groups=mesh['group'=2,'env'=16] {'env'}, use_global_device_ids=true, to_apply=%add | all-reduce | flops 192 | bytes 1536
  237.9 0.0 all-to-all-done
  237.9 0.1 all_to_all.17
  238.0 0.0 copy-start
  238.1 0.9 convolution_reduce_fusion
  238.9 0.0 copy-done
  (5 shorter events, 0.0 us)
Async XLA Ops:
  7.2 148.6 %copy-start.1 = (bf16[512,1024]{1,0:T(8,128)(2,1)S(1)}, bf16[512,1024]{1,0:T(8,128)(2,1)}, u32[]{:S(2)}) copy-start(bf16[512,1024]{1,0:T(8,128)(2,1)} %param.4) | copy-start | bytes 3145732
  7.2 138.7 %all-gather.2.cloned.1.call-start = ((), (), s32[]{:S(2)}) async-start(), calls=%async_computation.1 | async-start | bytes 27852800 | tf_op jit(solution)/shard_map/all_gather | solution.py:33
  180.7 21.4 %copy-start.3 = (u32[32]{0:T(128)S(1)}, u32[32]{0:T(128)}, u32[]{:S(2)}) copy-start(u32[32]{0:T(128)} %constant.13) | copy-start | bytes 388
  180.7 22.7 %copy-start.2 = (f32[12]{0:T(128)S(1)}, f32[12]{0:T(128)}, u32[]{:S(2)}) copy-start(f32[12]{0:T(128)} %param.7) | copy-start | bytes 148
  197.5 40.4 %all-to-all-start = ((bf16[12,16,800]{2,0,1:T(8,128)(2,1)}), bf16[12,16,800]{2,0,1:T(8,128)(2,1)S(1)}, u32[]{:S(2)}, u32[]{:S(2)}) async-start(bf16[12,16,800]{2,0,1:T(8,128)(2,1)} %copy.7), calls=%async_computation | async-start | bytes 917504 | tf_op jit(solution)/shard_map/all_to_all | solution.py:37
  238.0 0.9 copy-start
Sparse Core Ops, SparseCore 0:
  9.6 136.2 all-gather.1
where the time goes:
time: 246 us
  waiting for transfers between devices  136 us (55%)
  matrix products  41.2 us (17%)
  blocking collectives  34.2 us (14%)
  between operations  14.8 us (6%)
  other arithmetic  12.9 us (5%)
  starting transfers between devices  4.74 us (2%)
    all_gather x1, waiting for transfers between devices, on_device(): block_rows = lax.all_gather(sparse_points, 'env', axis=0, tiled=True)  135 us
    unnamed x1, blocking collectives  34.2 us
    dot_general x1, matrix products, kernel_block(): lax.dot_general(atom_rows, sparse_rows, (((1,), (1,)), ((), ())), preferr...  25 us
    dot_general x1, matrix products, on_device(): config_part = jnp.dot(onehot, kernel, precision=lax.Precision.HIGHEST)  15.3 us
    reduce_sum x2, other arithmetic, inverse_norms(): return lax.rsqrt(jnp.sum(values_f * values_f, axis=1) + EPS)  11.4 us
  transfers between devices with their start and end apart: 2, of which 1 were waited for; matrix products, arithmetic and copies ran while one was open for 2% of the time, Pallas kernels for 0%

commit v1 on v0

--- a/solution.py
+++ b/solution.py
@@ -1,9 +1,15 @@
+import functools
+
 import jax
 import jax.numpy as jnp
 from jax import lax
+from jax.experimental import pallas as pl
+from jax.experimental.pallas import tpu as pltpu
 from jax.sharding import PartitionSpec as P
 
 EPS = 1e-06
+LANES = 128
+VMEM_BUDGET = 44 * 1024 * 1024
 
 
 def inverse_norms(values):
@@ -20,7 +26,7 @@
     return squared * squared
 
 
-def on_device(descriptors, sparse_points, counts, energies):
+def gather_sparse(descriptors, sparse_points, counts, energies):
     atoms_here = descriptors.shape[0]
     all_energies = lax.all_gather(energies, "env", axis=0, tiled=True)
     inv_atoms = inverse_norms(descriptors)
@@ -41,7 +47,258 @@
     return (design, normal_rhs)
 
 
+def ring_kernel(
+    n_env, chunks, a_hbm, s_hbm, counts_ref, energies_ref, design_ref, rhs_ref,
+    blocks, s_ref, metas, inv_s, sums, rhs_acc,
+    own_sem, sparse_sem, send_next, send_side, recv_next, recv_side,
+    meta_send_next, meta_send_side, meta_recv_next, meta_recv_side,
+):
+    ring = n_env // 2
+    column = ring // 2
+    n_atoms, depth = a_hbm.shape
+    n_sparse = s_ref.shape[0]
+    n_conf = counts_ref.shape[1]
+    rows = n_atoms // chunks
+
+    me = lax.axis_index("env")
+    core = me % 2
+    y = (me // 2) % 2
+    z = me // 4
+    place = z * (1 - y) + (2 * column - 1 - z) * y
+    step_way = 1 - 2 * core
+
+    def device_at(p, c):
+        py = p // column
+        pz = p * (1 - py) + (2 * column - 1 - p) * py
+        return pz * 4 + py * 2 + c
+
+    nxt = device_at((place + step_way + ring) % ring, core)
+    prv = device_at((place - step_way + ring) % ring, core)
+    side = me + 1 - 2 * core
+
+    barrier = pltpu.get_barrier_semaphore()
+    for other in (nxt, prv, side):
+        pl.semaphore_signal(
+            barrier, inc=1, device_id={"env": other}, device_id_type=pl.DeviceIdType.MESH
+        )
+
+    own = [
+        pltpu.make_async_copy(
+            a_hbm.at[pl.ds(j * rows, rows)], blocks.at[0, pl.ds(j * rows, rows)], own_sem.at[j]
+        )
+        for j in range(chunks)
+    ]
+    for copy in own:
+        copy.start()
+    sparse = pltpu.make_async_copy(s_hbm, s_ref, sparse_sem)
+    sparse.start()
+
+    def remote(src, dst, send, recv, device):
+        return pltpu.make_async_remote_copy(
+            src_ref=src, dst_ref=dst, send_sem=send, recv_sem=recv,
+            device_id={"env": device}, device_id_type=pl.DeviceIdType.MESH,
+        )
+
+    def piece(k, j):
+        return blocks.at[k, pl.ds(j * rows, rows)]
+
+    def to_next(k, j):
+        return remote(piece(k, j), piece(k + 1, j), send_next.at[k, j], recv_next.at[k + 1, j], nxt)
+
+    def to_side(k, j):
+        return remote(piece(k, j), piece(ring + k, j), send_side.at[k, j], recv_side.at[k, j], side)
+
+    def meta_next(k):
+        return remote(metas.at[k], metas.at[k + 1], meta_send_next.at[k], meta_recv_next.at[k + 1], nxt)
+
+    def meta_side(k):
+        return remote(metas.at[k], metas.at[ring + k], meta_send_side.at[k], meta_recv_side.at[k], side)
+
+    pl.semaphore_wait(barrier, 3)
+    for j in range(chunks):
+        own[j].wait()
+        to_next(0, j).start()
+        to_side(0, j).start()
+
+    ones = jnp.ones((8, depth), jnp.bfloat16)
+    for j in range(chunks):
+        values = blocks[0, j * rows:(j + 1) * rows, :].astype(jnp.float32)
+        squares = values * values
+        high = squares.astype(jnp.bfloat16)
+        low = (squares - high.astype(jnp.float32)).astype(jnp.bfloat16)
+        contract = (((1,), (1,)), ((), ()))
+        total = lax.dot_general(ones, high, contract, preferred_element_type=jnp.float32)
+        total += lax.dot_general(ones, low, contract, preferred_element_type=jnp.float32)
+        metas[0, :, j * rows:(j + 1) * rows] = lax.rsqrt(total + EPS)
+    padded = jnp.concatenate(
+        [counts_ref[...].astype(jnp.float32), jnp.zeros((1, LANES - n_conf), jnp.float32)], axis=1
+    )
+    lower = lax.broadcasted_iota(jnp.int32, (LANES, LANES), 0)
+    upper = lax.broadcasted_iota(jnp.int32, (LANES, LANES), 1)
+    ends = jnp.dot(
+        jnp.broadcast_to(padded, (8, LANES)).astype(jnp.bfloat16),
+        (lower <= upper).astype(jnp.bfloat16),
+        preferred_element_type=jnp.float32,
+    )[0:1]
+    metas[0, 1:2, 0:LANES] = ends - padded
+    metas[0, 2:3, 0:LANES] = ends
+    metas[0, 3:4, 0:LANES] = jnp.concatenate(
+        [energies_ref[...], jnp.zeros((1, LANES - n_conf), jnp.float32)], axis=1
+    )
+    meta_next(0).start()
+    meta_side(0).start()
+
+    sparse.wait()
+    values = s_ref[...].astype(jnp.float32)
+    norms = lax.rsqrt(jnp.sum(values * values, axis=1, keepdims=True) + EPS)
+    inv_s[...] = jnp.broadcast_to(norms, inv_s.shape)
+    rhs_acc[...] = jnp.zeros_like(rhs_acc)
+    sums[...] = jnp.zeros_like(sums)
+
+    def part(way, slot, j):
+        products = lax.dot_general(
+            s_ref[...], blocks[slot, j * rows:(j + 1) * rows, :], (((1,), (1,)), ((), ())),
+            preferred_element_type=jnp.float32,
+        )
+        cosine = products * metas[slot, 0:1, j * rows:(j + 1) * rows] * inv_s[:, 0:1]
+        squared = cosine * cosine
+        kernel = squared * squared
+        high = kernel.astype(jnp.bfloat16)
+        low = (kernel - high.astype(jnp.float32)).astype(jnp.bfloat16)
+        at = (lax.broadcasted_iota(jnp.int32, (rows, LANES), 0) + j * rows).astype(jnp.float32)
+        inside = (at >= metas[slot, 1:2, 0:LANES]) & (at < metas[slot, 2:3, 0:LANES])
+        onehot = jnp.where(inside, 1.0, 0.0).astype(jnp.bfloat16)
+        total = jnp.dot(high, onehot, preferred_element_type=jnp.float32)
+        total += jnp.dot(low, onehot, preferred_element_type=jnp.float32)
+        if j == 0:
+            sums[way, 0:n_sparse] = total
+        else:
+            sums[way, 0:n_sparse] += total
+
+    def finish(way, slot, source):
+        rounded = sums[way].astype(jnp.bfloat16).astype(jnp.float32)
+        rhs_acc[...] += rounded * metas[slot, 3:4, 0:LANES]
+        turned = rounded.T[0:n_conf, 0:n_sparse]
+        design_ref[source] = turned.astype(jnp.bfloat16)
+
+    def own_source(k):
+        return device_at((place + ring * ring - k * step_way) % ring, core)
+
+    def side_source(k):
+        return device_at((place + ring * ring + k * step_way) % ring, 1 - core)
+
+    def use(k, j):
+        part(0, k, j)
+        if j == 0:
+            meta_side(k).wait_recv()
+        to_side(k, j).wait_recv()
+        part(1, ring + k, j)
+        if j == chunks - 1:
+            finish(0, k, own_source(k))
+            finish(1, ring + k, side_source(k))
+
+    def step(k, last):
+        for j in range(chunks):
+            to_next(k - 1, j).wait_recv()
+            if not last:
+                to_next(k, j).start()
+            to_side(k, j).start()
+            if j == 0:
+                meta_next(k - 1).wait_recv()
+                if not last:
+                    meta_next(k).start()
+                meta_side(k).start()
+                use(k - 1, chunks - 1)
+            else:
+                use(k, j - 1)
+
+    for j in range(chunks - 1):
+        use(0, j)
+
+    @pl.loop(1, ring - 1)
+    def _(k):
+        step(k, False)
+
+    step(ring - 1, True)
+    use(ring - 1, chunks - 1)
+    rhs_ref[...] = jnp.sum(rhs_acc[...].T, axis=0, keepdims=True)[:, 0:n_sparse]
+
+    @pl.loop(0, ring)
+    def _(k):
+        for j in range(chunks):
+            to_side(k, j).wait_send()
+        meta_side(k).wait_send()
+
+    @pl.loop(0, ring - 1)
+    def _(k):
+        for j in range(chunks):
+            to_next(k, j).wait_send()
+        meta_next(k).wait_send()
+
+
+def gather_atoms(n_env, descriptors, sparse_points, counts, energies):
+    n_atoms, depth = descriptors.shape
+    n_sparse = sparse_points.shape[0]
+    n_conf = counts.shape[1]
+    ring = n_env // 2
+    chunks = 2
+    wide = pl.cdiv(n_sparse, LANES) * LANES
+    dma = pltpu.SemaphoreType.DMA
+    design, rhs = pl.pallas_call(
+        functools.partial(ring_kernel, n_env, chunks),
+        out_shape=(
+            jax.ShapeDtypeStruct((n_env, n_conf, n_sparse), jnp.bfloat16),
+            jax.ShapeDtypeStruct((1, n_sparse), jnp.float32),
+        ),
+        in_specs=[
+            pl.BlockSpec(memory_space=pl.ANY),
+            pl.BlockSpec(memory_space=pl.ANY),
+            pl.BlockSpec(memory_space=pltpu.VMEM),
+            pl.BlockSpec(memory_space=pltpu.VMEM),
+        ],
+        out_specs=(
+            pl.BlockSpec(memory_space=pltpu.VMEM),
+            pl.BlockSpec(memory_space=pltpu.VMEM),
+        ),
+        scratch_shapes=[
+            pltpu.VMEM((n_env, n_atoms, depth), jnp.bfloat16),
+            pltpu.VMEM((n_sparse, depth), jnp.bfloat16),
+            pltpu.VMEM((n_env, 8, n_atoms), jnp.float32),
+            pltpu.VMEM((n_sparse, LANES), jnp.float32),
+            pltpu.VMEM((2, wide, LANES), jnp.float32),
+            pltpu.VMEM((wide, LANES), jnp.float32),
+            dma((chunks,)),
+            dma,
+            dma((ring, chunks)),
+            dma((ring, chunks)),
+            dma((ring, chunks)),
+            dma((ring, chunks)),
+            dma((ring,)),
+            dma((ring,)),
+            dma((ring,)),
+            dma((ring,)),
+        ],
+        compiler_params=pltpu.CompilerParams(
+            collective_id=0, has_side_effects=True, vmem_limit_bytes=VMEM_BUDGET
+        ),
+        cost_estimate=pl.CostEstimate(
+            flops=2 * n_env * n_atoms * n_sparse * depth,
+            bytes_accessed=2 * (n_atoms + n_sparse) * depth,
+            transcendentals=0,
+        ),
+    )(descriptors, sparse_points, counts, energies.reshape(1, n_conf))
+    return (design.reshape(n_env * n_conf, n_sparse), rhs.reshape(n_sparse))
+
+
 def solution(mesh):
+    n_env = mesh.shape["env"]
+
+    def on_device(descriptors, sparse_points, counts, energies):
+        gathered = 2 * n_env * descriptors.shape[0] * descriptors.shape[1]
+        if n_env % 4 == 0 and n_env > 4 and gathered <= VMEM_BUDGET // 2:
+            return gather_atoms(n_env, descriptors, sparse_points, counts, energies)
+        return gather_sparse(descriptors, sparse_points, counts, energies)
+
     return jax.shard_map(
         on_device,
         mesh=mesh,

time: 246 us -> 98.9 us (0.40)
  waiting for transfers between devices: 136 us -> 0 us
  Pallas kernels: 0 us -> 92.6 us
  matrix products: 41.2 us -> 0 us
  blocking collectives: 34.2 us -> 0 us
  between operations: 14.8 us -> 0.65 us
  other arithmetic: 12.9 us -> 0.61 us
  starting transfers between devices: 4.74 us -> 0 us
  local copies, waits for them, and re-layouts: 2.37 us -> 4.83 us
    all_gather x1 -> x0, waiting for transfers between devices: 135 us -> none  [on_device(): block_rows = lax.all_gather(sparse_points, 'env', axis=0, tiled=True)]
    pallas_call x0 -> x1, Pallas kernels: none -> 92.6 us  [gather_atoms(): pl.pallas_call(functools.partial(ring_kernel, n_env, chunks), out_shape=(...]
    dot_general x3 -> x0, matrix products: 41.2 us -> none  [the longest x1 25 us: kernel_block(): lax.dot_general(atom_rows, sparse_rows, (((1,), (1,)), ((), ())), preferr...]
    unnamed x1 -> x0, blocking collectives: 34.2 us -> none
    reduce_sum x2 -> x0, other arithmetic: 11.4 us -> none  [inverse_norms(): return lax.rsqrt(jnp.sum(values_f * values_f, axis=1) + EPS)]
    all_to_all x1 -> x0, starting transfers between devices: 4.7 us -> none  [on_device(): lax.all_to_all(config_part.astype(jnp.bfloat16), 'env', split_axis=1, con...]
    unnamed x11 -> x8, local copies, waits for them, and re-layouts: 0.85 us -> 3.96 us
  transfers between devices with their start and end apart: 2 -> 0, of which waited for: 1 -> 0; matrix products, arithmetic and copies ran while one was open for 2% -> 0% of each run, Pallas kernels for 0% -> 0%
where the time goes in v1:
time: 98.9 us; the launch traced here: 98.7 us
  Pallas kernels  92.6 us (94%)
  local copies, waits for them, and re-layouts  4.83 us (5%)
    pallas_call x1, Pallas kernels, gather_atoms(): pl.pallas_call(functools.partial(ring_kernel, n_env, chunks), out_shape=(...  92.6 us
    unnamed x8, local copies, waits for them, and re-layouts  3.96 us

profile of v1, /device:TPU:0, one launch (start us, length us, event | category | flops | bytes accessed | tf_op | source)
XLA Modules:
  0.0 98.7 jit_solution(3521979428397347151)
XLA Ops:
  0.6 0.0 copy-start
  0.6 1.4 %copy-done = bf16[800,1024]{1,0:T(8,128)(2,1)S(1)} copy-done((bf16[800,1024]{1,0:T(8,128)(2,1)S(1)}, bf16[800,1024]{1,0:T(8,128)(2,1)}, u32[]{:S(2)}) %copy-start) | copy-done | bytes 1638424
  2.1 0.0 copy-start.1
  2.1 1.2 %copy-done.1 = bf16[512,1024]{1,0:T(8,128)(2,1)S(1)} copy-done((bf16[512,1024]{1,0:T(8,128)(2,1)S(1)}, bf16[512,1024]{1,0:T(8,128)(2,1)}, u32[]{:S(2)}) %copy-start.1) | copy-done | bytes 1048600
  3.3 0.0 copy-start.2
  3.3 0.7 copy-done.2
  3.9 0.0 copy-start.3
  3.9 0.7 copy-done.3
  4.6 92.6 %shard_map.59 = (bf16[16,12,800]{2,1,0:T(8,128)(2,1)S(1)}, f32[1,800]{1,0:T(1,128)S(1)}) custom-call(bf16[512,1024]{1,0:T(8,128)(2,1)S(1)} %copy-done.1, bf16[800,1024]{1,0:T(8,128)(2,1)S(1)} %copy-done, s32[1,12]{1,0:T(1,128)S(1)} %copy-done.2, f32[1,12]{1,0:T(1,128)S(1)} %bitcast.1), custom_call_target="tpu_custom_call" | custom-call | flops 13421772800 | bytes 2686976 | tf_op jit(solution)/shard_map/pallas_call | solution.py:247
  97.2 0.9 reshape.14
  98.1 0.6 reduce
Async XLA Ops:
  0.6 1.4 %copy-start = (bf16[800,1024]{1,0:T(8,128)(2,1)S(1)}, bf16[800,1024]{1,0:T(8,128)(2,1)}, u32[]{:S(2)}) copy-start(bf16[800,1024]{1,0:T(8,128)(2,1)} %s_hbm.1) | copy-start | bytes 4915204
  2.1 1.2 %copy-start.1 = (bf16[512,1024]{1,0:T(8,128)(2,1)S(1)}, bf16[512,1024]{1,0:T(8,128)(2,1)}, u32[]{:S(2)}) copy-start(bf16[512,1024]{1,0:T(8,128)(2,1)} %a_hbm.1) | copy-start | bytes 3145732
  3.3 0.7 copy-start.2
  3.9 0.7 copy-start.3

commit v2 on v0

--- a/solution.py
+++ b/solution.py
@@ -1,9 +1,15 @@
+import functools
+
 import jax
 import jax.numpy as jnp
 from jax import lax
+from jax.experimental import pallas as pl
+from jax.experimental.pallas import tpu as pltpu
 from jax.sharding import PartitionSpec as P
 
 EPS = 1e-06
+LANES = 128
+VMEM_BUDGET = 44 * 1024 * 1024
 
 
 def inverse_norms(values):
@@ -20,7 +26,7 @@
     return squared * squared
 
 
-def on_device(descriptors, sparse_points, counts, energies):
+def gather_sparse(descriptors, sparse_points, counts, energies):
     atoms_here = descriptors.shape[0]
     all_energies = lax.all_gather(energies, "env", axis=0, tiled=True)
     inv_atoms = inverse_norms(descriptors)
@@ -41,7 +47,390 @@
     return (design, normal_rhs)
 
 
+def block_kernel(
+    cuts, chunks, a_hbm, s_hbm, counts_hbm, energies_hbm, design_ref, rhs_ref,
+    blocks, metas, sparse, other, inv_own, inv_other, sum_own, sum_other, out_other, in_other,
+    row_energies, counts_ref, energies_ref,
+    own_sem, small_sem, recv, send_y, send_side, send_part, send_cross,
+    s_send, s_recv, r_send, r_recv, e_send, e_recv,
+):
+    n_atoms, depth = a_hbm.shape
+    n_sparse = s_hbm.shape[0]
+    n_conf = counts_hbm.shape[1]
+    rows = n_atoms // chunks
+    half = n_atoms // 2
+    META = chunks
+    items = [0, META] + list(range(1, chunks))
+
+    me = lax.axis_index("env")
+    core = me % 2
+    y = (me // 2) % 2
+    z = me // 4
+    inner_i = (z % 3 + 1) // 2
+    inner = inner_i == 1
+    outer = inner_i == 0
+    pair_z = z + 1 - 2 * (z % 2)
+    side = me + 1 - 2 * core
+    over = me + 2 - 4 * y
+    partner = pair_z * 4 + y * 2 + core
+    cross = (3 - z) * 4 + y * 2 + core
+    own = 9 * inner_i
+
+    barrier = pltpu.get_barrier_semaphore()
+
+    def greet(device):
+        pl.semaphore_signal(
+            barrier, inc=1, device_id={"env": device}, device_id_type=pl.DeviceIdType.MESH
+        )
+
+    for device in (side, over, partner):
+        greet(device)
+
+    @pl.when(inner)
+    def _():
+        greet(cross)
+
+    def piece(slot, item):
+        if item == META:
+            return metas.at[slot]
+        return blocks.at[slot, pl.ds(item * rows, rows)]
+
+    def remote(src, dst, send, arrive, device):
+        return pltpu.make_async_remote_copy(
+            src_ref=src, dst_ref=dst, send_sem=send, recv_sem=arrive,
+            device_id={"env": device}, device_id_type=pl.DeviceIdType.MESH,
+        )
+
+    def hand(src, dst, item, send, device):
+        return remote(piece(src, item), piece(dst, item), send.at[item], recv.at[dst, item], device)
+
+    def to_side(q, item):
+        return hand(q, 4 + q, item, send_side.at[q], side)
+
+    def to_over(q, item):
+        return hand(q, q + 1, item, send_y.at[q // 2], over)
+
+    def to_part(item):
+        return hand(own, 8 - 6 * inner_i, item, send_part, partner)
+
+    def to_cross(src, dst, item):
+        return hand(src, dst, item, send_cross.at[dst // 2], cross)
+
+    def arrived(slot, item):
+        remote(
+            piece(slot, item), piece(slot, item), send_part.at[item], recv.at[slot, item], side
+        ).wait_recv()
+
+    def s_rows(n):
+        return pl.ds(cuts[n], cuts[n + 1] - cuts[n])
+
+    def give_sparse(n):
+        return remote(s_hbm.at[s_rows(n)], other.at[s_rows(n)], s_send.at[n], s_recv.at[n], partner)
+
+    def give_sums(n):
+        return remote(
+            out_other.at[s_rows(n)], in_other.at[s_rows(n)], r_send.at[n], r_recv.at[n], partner
+        )
+
+    give_energies = remote(row_energies.at[0], row_energies.at[1], e_send, e_recv, partner)
+
+    local = [
+        pltpu.make_async_copy(a_hbm.at[pl.ds(j * rows, rows)], piece(own, j), own_sem.at[j])
+        for j in range(chunks)
+    ]
+    local_sparse = pltpu.make_async_copy(s_hbm, sparse, small_sem.at[0])
+    local_counts = pltpu.make_async_copy(counts_hbm, counts_ref, small_sem.at[1])
+    local_energies = pltpu.make_async_copy(energies_hbm, energies_ref, small_sem.at[2])
+    for copy in local + [local_counts, local_energies, local_sparse]:
+        copy.start()
+
+    def send_own(item):
+        to_part(item).start()
+
+        @pl.when(inner)
+        def _():
+            to_cross(own, 0, item).start()
+
+        @pl.when(outer)
+        def _():
+            to_over(0, item).start()
+            to_side(0, item).start()
+
+    pl.semaphore_wait(barrier, 3 + inner_i)
+    local[0].wait()
+    send_own(0)
+
+    for copy in local[1:]:
+        copy.wait()
+    ones = jnp.ones((8, depth), jnp.bfloat16)
+    contract = (((1,), (1,)), ((), ()))
+    for j in range(2):
+        values = blocks[own, j * half:(j + 1) * half, :].astype(jnp.float32)
+        squares = values * values
+        high = squares.astype(jnp.bfloat16)
+        low = (squares - high.astype(jnp.float32)).astype(jnp.bfloat16)
+        total = lax.dot_general(ones, high, contract, preferred_element_type=jnp.float32)
+        total += lax.dot_general(ones, low, contract, preferred_element_type=jnp.float32)
+        metas[own, :, j * half:(j + 1) * half] = lax.rsqrt(total + EPS)
+    local_counts.wait()
+    local_energies.wait()
+    down = lax.broadcasted_iota(jnp.int32, (LANES, LANES), 0)
+    along = lax.broadcasted_iota(jnp.int32, (LANES, LANES), 1) % 16
+    blank = jnp.zeros((1, LANES - n_conf), jnp.float32)
+
+    def spread(row, keep):
+        keep = jnp.where(keep & (along < n_conf), 1.0, 0.0)
+        return jnp.dot(
+            jnp.broadcast_to(jnp.concatenate([row, blank], axis=1), (8, LANES)), keep,
+            precision=lax.Precision.HIGHEST, preferred_element_type=jnp.float32,
+        )[0:1]
+
+    counts_f = counts_ref[...].astype(jnp.float32)
+    metas[own, 1:2, 0:LANES] = spread(counts_f, down < along)
+    metas[own, 2:3, 0:LANES] = spread(counts_f, down <= along)
+    metas[own, 3:4, 0:LANES] = spread(energies_ref[...], down == along)
+    for item in items[1:]:
+        send_own(item)
+
+    def scale_rows(points, inv, start, stop):
+        values = points[start:stop, :].astype(jnp.float32)
+        norms = lax.rsqrt(jnp.sum(values * values, axis=1, keepdims=True) + EPS)
+        inv[start:stop, :] = jnp.broadcast_to(norms, (stop - start, LANES))
+
+    local_sparse.wait()
+    scale_rows(sparse, inv_own, 0, n_sparse)
+    sum_own[...] = jnp.zeros_like(sum_own)
+    sum_other[...] = jnp.zeros_like(sum_other)
+    if in_other.shape[0] > n_sparse:
+        in_other[n_sparse:, :] = jnp.zeros((in_other.shape[0] - n_sparse, LANES), jnp.bfloat16)
+
+    def unit(points, inv, sums, start, stop, slot, u):
+        products = lax.dot_general(
+            points[start:stop, :], blocks[slot, u * half:(u + 1) * half, :], contract,
+            preferred_element_type=jnp.float32,
+        )
+        cosine = products * metas[slot, 0:1, u * half:(u + 1) * half] * inv[start:stop, 0:1]
+        squared = cosine * cosine
+        kernel = squared * squared
+        high = kernel.astype(jnp.bfloat16)
+        low = (kernel - high.astype(jnp.float32)).astype(jnp.bfloat16)
+        at = (lax.broadcasted_iota(jnp.int32, (half, LANES), 0) + u * half).astype(jnp.float32)
+        lane = lax.broadcasted_iota(jnp.int32, (half, LANES), 1)
+        inside = (at >= metas[slot, 1:2, 0:LANES]) & (at < metas[slot, 2:3, 0:LANES])
+        onehot = jnp.where(inside & (lane // 16 == slot), 1.0, 0.0).astype(jnp.bfloat16)
+        total = jnp.dot(high, onehot, preferred_element_type=jnp.float32)
+        total += jnp.dot(low, onehot, preferred_element_type=jnp.float32)
+        sums[start:stop, :] += total
+
+    def use_own(qs, u):
+        first, n = qs
+
+        @pl.loop(0, 2 * n)
+        def _(i):
+            unit(sparse, inv_own, sum_own, 0, n_sparse, first + i // 2 + 4 * (i % 2), u)
+
+    def use_other(part, qs):
+        first, n = qs
+
+        @pl.loop(0, 2 * n)
+        def _(i):
+            for u in range(2):
+                unit(
+                    other, inv_other, sum_other, cuts[part], cuts[part + 1],
+                    first + i // 2 + 4 * (i % 2), u,
+                )
+
+    def take_sparse(part):
+        give_sparse(part).wait_recv()
+        scale_rows(other, inv_other, cuts[part], cuts[part + 1])
+
+    def give_back(part):
+        out_other[s_rows(part)] = sum_other[s_rows(part)].astype(jnp.bfloat16)
+        give_sums(part).start()
+
+    for item in items:
+        @pl.when(inner)
+        def _():
+            arrived(0, item)
+            to_over(0, item).start()
+            to_side(0, item).start()
+            arrived(8, item)
+            to_cross(8, 2, item).start()
+
+        @pl.when(outer)
+        def _():
+            arrived(2, item)
+            to_over(2, item).start()
+            to_side(2, item).start()
+
+        arrived(1, item)
+        to_side(1, item).start()
+        arrived(4, item)
+        arrived(5, item)
+        if item == chunks // 2:
+            give_sparse(0).start()
+            use_own((0, 2), 0)
+        if item == chunks - 1:
+            give_sparse(1).start()
+
+    for item in items:
+        @pl.when(inner)
+        def _():
+            arrived(2, item)
+            to_over(2, item).start()
+            to_side(2, item).start()
+
+        arrived(6, item)
+        if item == chunks - 1:
+            use_own((2, 1), 1)
+            use_other(0, (2, 1))
+            take_sparse(1)
+            use_other(1, (0, 3))
+        arrived(3, item)
+        to_side(3, item).start()
+        if item == 0:
+            give_sparse(2).start()
+            use_own((0, 2), 1)
+        if item == 1:
+            give_sparse(3).start()
+            take_sparse(0)
+            use_other(0, (0, 2))
+        arrived(7, item)
+        if item == chunks // 2:
+            use_own((2, 2), 0)
+
+    use_own((3, 1), 1)
+    use_other(0, (3, 1))
+    give_back(0)
+    use_other(1, (3, 1))
+    give_back(1)
+
+    lanes = lax.broadcasted_iota(jnp.int32, (1, LANES), 1) // 16
+    mine = jnp.zeros((1, LANES), jnp.float32)
+    for slot in range(8):
+        mine += jnp.where(lanes == slot, metas[slot, 3:4, 0:LANES], 0.0)
+    row_energies[0] = jnp.broadcast_to(mine, (8, LANES))
+    give_energies.start()
+
+    def finish(rounded, energies, at_z, at_inner):
+        other_z = at_z + 1 - 2 * (at_z % 2)
+        near = at_z + at_inner * (3 - 2 * at_z)
+        far = other_z + at_inner * (3 - 2 * other_z)
+        turned = rounded.T
+        for slot in range(8):
+            q = slot % 4
+            from_z = near if q < 2 else far
+            from_y = y if q % 2 == 0 else 1 - y
+            from_core = core if slot < 4 else 1 - core
+            design_ref[from_z * 4 + from_y * 2 + from_core] = turned[
+                16 * slot:16 * slot + n_conf, 0:n_sparse
+            ].astype(jnp.bfloat16)
+        return jnp.sum((rounded * energies).T, axis=0, keepdims=True)[:, 0:n_sparse]
+
+    take_sparse(2)
+    use_other(2, (0, 4))
+    give_back(2)
+    rhs_ref[...] = finish(
+        sum_own[...].astype(jnp.bfloat16).astype(jnp.float32), mine, z, inner_i
+    )
+    take_sparse(3)
+    use_other(3, (0, 4))
+    give_back(3)
+
+    give_energies.wait_recv()
+    for part in range(len(cuts) - 1):
+        give_sums(part).wait_recv()
+    rhs_ref[...] += finish(
+        in_other[...].astype(jnp.float32), row_energies[1, 0:1, :], pair_z, 1 - inner_i
+    )
+
+    give_energies.wait_send()
+    for part in range(len(cuts) - 1):
+        give_sparse(part).wait_send()
+        give_sums(part).wait_send()
+    for item in items:
+        to_part(item).wait_send()
+        for q in range(4):
+            to_side(q, item).wait_send()
+        to_over(0, item).wait_send()
+        to_over(2, item).wait_send()
+
+        @pl.when(inner)
+        def _():
+            to_cross(own, 0, item).wait_send()
+            to_cross(8, 2, item).wait_send()
+
+
+def split_both(descriptors, sparse_points, counts, energies):
+    n_atoms, depth = descriptors.shape
+    n_sparse = sparse_points.shape[0]
+    n_conf = counts.shape[1]
+    n_env = 16
+    chunks = 4
+    unit = n_sparse // 6 // LANES * LANES
+    cuts = (0, 2 * unit, 4 * unit, 5 * unit, n_sparse)
+    parts = len(cuts) - 1
+    wide = pl.cdiv(n_sparse, LANES) * LANES
+    dma = pltpu.SemaphoreType.DMA
+    design, rhs = pl.pallas_call(
+        functools.partial(block_kernel, cuts, chunks),
+        out_shape=(
+            jax.ShapeDtypeStruct((n_env, n_conf, n_sparse), jnp.bfloat16),
+            jax.ShapeDtypeStruct((1, n_sparse), jnp.float32),
+        ),
+        in_specs=[pl.BlockSpec(memory_space=pltpu.HBM)] * 4,
+        out_specs=(
+            pl.BlockSpec(memory_space=pltpu.VMEM),
+            pl.BlockSpec(memory_space=pltpu.VMEM),
+        ),
+        scratch_shapes=[
+            pltpu.VMEM((10, n_atoms, depth), jnp.bfloat16),
+            pltpu.VMEM((10, 8, n_atoms), jnp.float32),
+            pltpu.VMEM((n_sparse, depth), jnp.bfloat16),
+            pltpu.VMEM((n_sparse, depth), jnp.bfloat16),
+            pltpu.VMEM((n_sparse, LANES), jnp.float32),
+            pltpu.VMEM((n_sparse, LANES), jnp.float32),
+            pltpu.VMEM((wide, LANES), jnp.float32),
+            pltpu.VMEM((wide, LANES), jnp.float32),
+            pltpu.VMEM((n_sparse, LANES), jnp.bfloat16),
+            pltpu.VMEM((wide, LANES), jnp.bfloat16),
+            pltpu.VMEM((2, 8, LANES), jnp.float32),
+            pltpu.VMEM((1, n_conf), jnp.int32),
+            pltpu.VMEM((1, n_conf), jnp.float32),
+            dma((chunks,)),
+            dma((3,)),
+            dma((9, chunks + 1)),
+            dma((2, chunks + 1)),
+            dma((4, chunks + 1)),
+            dma((chunks + 1,)),
+            dma((2, chunks + 1)),
+            dma((parts,)),
+            dma((parts,)),
+            dma((parts,)),
+            dma((parts,)),
+            dma,
+            dma,
+        ],
+        compiler_params=pltpu.CompilerParams(
+            collective_id=0, has_side_effects=True, vmem_limit_bytes=VMEM_BUDGET
+        ),
+        cost_estimate=pl.CostEstimate(
+            flops=2 * n_env * n_atoms * n_sparse * depth,
+            bytes_accessed=2 * (n_atoms + n_sparse) * depth,
+            transcendentals=0,
+        ),
+    )(descriptors, sparse_points, counts, energies.reshape(1, n_conf))
+    return (design.reshape(n_env * n_conf, n_sparse), rhs.reshape(n_sparse))
+
+
 def solution(mesh):
+    n_env = mesh.shape["env"]
+
+    def on_device(descriptors, sparse_points, counts, energies):
+        if n_env == 16 and counts.shape[1] <= 16 and sparse_points.shape[0] >= 6 * LANES:
+            return split_both(descriptors, sparse_points, counts, energies)
+        return gather_sparse(descriptors, sparse_points, counts, energies)
+
     return jax.shard_map(
         on_device,
         mesh=mesh,

time: 246 us -> 139 us (0.57)
  waiting for transfers between devices: 136 us -> 0 us
  Pallas kernels: 0 us -> 133 us
  matrix products: 41.2 us -> 0 us
  blocking collectives: 34.2 us -> 0 us
  between operations: 14.8 us -> 0.65 us
  other arithmetic: 12.9 us -> 0.61 us
  starting transfers between devices: 4.74 us -> 0 us
  local copies, waits for them, and re-layouts: 2.37 us -> 4.83 us
    all_gather x1 -> x0, waiting for transfers between devices: 135 us -> none  [on_device(): block_rows = lax.all_gather(sparse_points, 'env', axis=0, tiled=True)]
    pallas_call x0 -> x1, Pallas kernels: none -> 133 us  [split_both(): pl.pallas_call(functools.partial(block_kernel, cuts, chunks), out_shape=(...]
    dot_general x3 -> x0, matrix products: 41.2 us -> none  [the longest x1 25 us: kernel_block(): lax.dot_general(atom_rows, sparse_rows, (((1,), (1,)), ((), ())), preferr...]
    unnamed x1 -> x0, blocking collectives: 34.2 us -> none
    reduce_sum x2 -> x0, other arithmetic: 11.4 us -> none  [inverse_norms(): return lax.rsqrt(jnp.sum(values_f * values_f, axis=1) + EPS)]
    all_to_all x1 -> x0, starting transfers between devices: 4.7 us -> none  [on_device(): lax.all_to_all(config_part.astype(jnp.bfloat16), 'env', split_axis=1, con...]
    unnamed x11 -> x8, local copies, waits for them, and re-layouts: 0.85 us -> 3.96 us
  transfers between devices with their start and end apart: 2 -> 0, of which waited for: 1 -> 0; matrix products, arithmetic and copies ran while one was open for 2% -> 0% of each run, Pallas kernels for 0% -> 0%
where the time goes in v2:
time: 139 us
  Pallas kernels  133 us (96%)
  local copies, waits for them, and re-layouts  4.83 us (3%)
    pallas_call x1, Pallas kernels, split_both(): pl.pallas_call(functools.partial(block_kernel, cuts, chunks), out_shape=(...  133 us
    unnamed x8, local copies, waits for them, and re-layouts  3.96 us

profile of v2, /device:TPU:0, one launch (start us, length us, event | category | flops | bytes accessed | tf_op | source)
XLA Modules:
  0.0 139.3 jit_solution(4271215834290173958)
XLA Ops:
  0.6 0.0 copy-start
  0.6 1.4 %copy-done = bf16[800,1024]{1,0:T(8,128)(2,1)S(1)} copy-done((bf16[800,1024]{1,0:T(8,128)(2,1)S(1)}, bf16[800,1024]{1,0:T(8,128)(2,1)}, u32[]{:S(2)}) %copy-start) | copy-done | bytes 1638424
  2.1 0.0 copy-start.1
  2.1 1.2 copy-done.1
  3.3 0.0 copy-start.2
  3.3 0.7 copy-done.2
  3.9 0.0 copy-start.3
  3.9 0.7 copy-done.3
  4.6 133.2 %shard_map.59 = (bf16[16,12,800]{2,1,0:T(8,128)(2,1)S(1)}, f32[1,800]{1,0:T(1,128)S(1)}) custom-call(bf16[512,1024]{1,0:T(8,128)(2,1)S(1)} %copy-done.1, bf16[800,1024]{1,0:T(8,128)(2,1)S(1)} %copy-done, s32[1,12]{1,0:T(1,128)S(1)} %copy-done.2, f32[1,12]{1,0:T(1,128)S(1)} %bitcast.1), custom_call_target="tpu_custom_call" | custom-call | flops 13421772800 | bytes 2686976 | tf_op jit(solution)/shard_map/pallas_call | solution.py:375
  137.8 0.9 reshape.14
  138.7 0.6 reduce
Async XLA Ops:
  0.6 1.4 %copy-start = (bf16[800,1024]{1,0:T(8,128)(2,1)S(1)}, bf16[800,1024]{1,0:T(8,128)(2,1)}, u32[]{:S(2)}) copy-start(bf16[800,1024]{1,0:T(8,128)(2,1)} %s_hbm.1) | copy-start | bytes 4915204
  2.1 1.2 copy-start.1
  3.3 0.7 copy-start.2
  3.9 0.7 copy-start.3

commit v3 on v2

--- a/solution.py
+++ b/solution.py
@@ -61,6 +61,7 @@
     half = n_atoms // 2
     META = chunks
     items = [0, META] + list(range(1, chunks))
+    last = chunks - 1
 
     me = lax.axis_index("env")
     core = me % 2
@@ -189,8 +190,8 @@
     metas[own, 1:2, 0:LANES] = spread(counts_f, down < along)
     metas[own, 2:3, 0:LANES] = spread(counts_f, down <= along)
     metas[own, 3:4, 0:LANES] = spread(energies_ref[...], down == along)
-    for item in items[1:]:
-        send_own(item)
+    send_own(META)
+    send_own(1)
 
     def scale_rows(points, inv, start, stop):
         values = points[start:stop, :].astype(jnp.float32)
@@ -204,41 +205,39 @@
     if in_other.shape[0] > n_sparse:
         in_other[n_sparse:, :] = jnp.zeros((in_other.shape[0] - n_sparse, LANES), jnp.bfloat16)
 
-    def unit(points, inv, sums, start, stop, slot, u):
+    def unit(points, inv, sums, start, stop, slot, first, end):
         products = lax.dot_general(
-            points[start:stop, :], blocks[slot, u * half:(u + 1) * half, :], contract,
+            points[start:stop, :], blocks[slot, first:end, :], contract,
             preferred_element_type=jnp.float32,
         )
-        cosine = products * metas[slot, 0:1, u * half:(u + 1) * half] * inv[start:stop, 0:1]
+        scale = jnp.concatenate([inv[start:stop, :]] * ((end - first) // LANES), axis=1)
+        cosine = products * metas[slot, 0:1, first:end] * scale
         squared = cosine * cosine
         kernel = squared * squared
         high = kernel.astype(jnp.bfloat16)
         low = (kernel - high.astype(jnp.float32)).astype(jnp.bfloat16)
-        at = (lax.broadcasted_iota(jnp.int32, (half, LANES), 0) + u * half).astype(jnp.float32)
-        lane = lax.broadcasted_iota(jnp.int32, (half, LANES), 1)
+        at = (lax.broadcasted_iota(jnp.int32, (end - first, LANES), 0) + first).astype(jnp.float32)
+        lane = lax.broadcasted_iota(jnp.int32, (end - first, LANES), 1)
         inside = (at >= metas[slot, 1:2, 0:LANES]) & (at < metas[slot, 2:3, 0:LANES])
         onehot = jnp.where(inside & (lane // 16 == slot), 1.0, 0.0).astype(jnp.bfloat16)
         total = jnp.dot(high, onehot, preferred_element_type=jnp.float32)
         total += jnp.dot(low, onehot, preferred_element_type=jnp.float32)
         sums[start:stop, :] += total
 
-    def use_own(qs, u):
-        first, n = qs
+    def use_own(q, n, first=0, end=None):
+        stop = n_atoms if end is None else end
 
         @pl.loop(0, 2 * n)
         def _(i):
-            unit(sparse, inv_own, sum_own, 0, n_sparse, first + i // 2 + 4 * (i % 2), u)
-
-    def use_other(part, qs):
-        first, n = qs
-
+            unit(sparse, inv_own, sum_own, 0, n_sparse, q + i // 2 + 4 * (i % 2), first, stop)
+
+    def use_other(part, upto, q, n):
         @pl.loop(0, 2 * n)
         def _(i):
-            for u in range(2):
-                unit(
-                    other, inv_other, sum_other, cuts[part], cuts[part + 1],
-                    first + i // 2 + 4 * (i % 2), u,
-                )
+            unit(
+                other, inv_other, sum_other, cuts[part], cuts[upto], q + i // 2 + 4 * (i % 2),
+                0, n_atoms,
+            )
 
     def take_sparse(part):
         give_sparse(part).wait_recv()
@@ -248,61 +247,92 @@
         out_other[s_rows(part)] = sum_other[s_rows(part)].astype(jnp.bfloat16)
         give_sums(part).start()
 
-    for item in items:
+    def items_of(j):
+        return [0, META] if j == 0 else [j]
+
+    def second_wave(j):
+        for item in items_of(j):
+            @pl.when(inner)
+            def _():
+                to_cross(8, 2, item).start()
+
+            @pl.when(outer)
+            def _():
+                to_over(2, item).start()
+
+    def pass_aside(q, j):
+        for item in items_of(j):
+            arrived(q, item)
+            to_side(q, item).start()
+
+    def aside(q, j):
+        for item in items_of(j):
+            arrived(4 + q, item)
+
+    for j in range(chunks):
+        for item in items_of(j):
+            @pl.when(inner)
+            def _():
+                arrived(0, item)
+                to_over(0, item).start()
+                to_side(0, item).start()
+                arrived(8, item)
+
+            @pl.when(outer)
+            def _():
+                arrived(2, item)
+                to_side(2, item).start()
+
+        if j + 2 < chunks:
+            send_own(j + 2)
+        else:
+            second_wave(j + 2 - chunks)
+            give_sparse(j + 2 - chunks).start()
+        if j > 0:
+            pass_aside(1, j - 1)
+
+    for j in range(chunks):
+        aside(0, j)
+    use_own(0, 1)
+
+    for j in range(chunks):
         @pl.when(inner)
         def _():
-            arrived(0, item)
-            to_over(0, item).start()
-            to_side(0, item).start()
-            arrived(8, item)
-            to_cross(8, 2, item).start()
-
-        @pl.when(outer)
-        def _():
-            arrived(2, item)
-            to_over(2, item).start()
-            to_side(2, item).start()
-
-        arrived(1, item)
-        to_side(1, item).start()
-        arrived(4, item)
-        arrived(5, item)
-        if item == chunks // 2:
-            give_sparse(0).start()
-            use_own((0, 2), 0)
-        if item == chunks - 1:
-            give_sparse(1).start()
-
-    for item in items:
-        @pl.when(inner)
-        def _():
-            arrived(2, item)
-            to_over(2, item).start()
-            to_side(2, item).start()
-
-        arrived(6, item)
-        if item == chunks - 1:
-            use_own((2, 1), 1)
-            use_other(0, (2, 1))
-            take_sparse(1)
-            use_other(1, (0, 3))
-        arrived(3, item)
-        to_side(3, item).start()
-        if item == 0:
-            give_sparse(2).start()
-            use_own((0, 2), 1)
-        if item == 1:
-            give_sparse(3).start()
+            for item in items_of(j):
+                arrived(2, item)
+                to_over(2, item).start()
+                to_side(2, item).start()
+
+        if j + 2 < chunks:
+            second_wave(j + 2)
+        else:
+            give_sparse(j).start()
+        if j == 0:
+            pass_aside(1, last)
+            for i in range(chunks):
+                aside(1, i)
+            use_own(1, 1)
+        else:
+            pass_aside(3, j - 1)
+        if j == 1:
             take_sparse(0)
-            use_other(0, (0, 2))
-        arrived(7, item)
-        if item == chunks // 2:
-            use_own((2, 2), 0)
-
-    use_own((3, 1), 1)
-    use_other(0, (3, 1))
+            use_other(0, 1, 0, 2)
+        if j == 2:
+            for i in range(2):
+                aside(2, i)
+            use_own(2, 1, 0, half)
+    for j in range(2, chunks):
+        aside(2, j)
+    use_own(2, 1, half)
+    use_other(0, 1, 2, 1)
+    pass_aside(3, last)
+    take_sparse(1)
+    use_other(1, 2, 0, 3)
+    for j in range(chunks):
+        aside(3, j)
+    use_own(3, 1)
+    use_other(0, 2, 3, 1)
     give_back(0)
-    use_other(1, (3, 1))
     give_back(1)
 
     lanes = lax.broadcasted_iota(jnp.int32, (1, LANES), 1) // 16
@@ -328,14 +358,13 @@
         return jnp.sum((rounded * energies).T, axis=0, keepdims=True)[:, 0:n_sparse]
 
     take_sparse(2)
-    use_other(2, (0, 4))
+    take_sparse(3)
+    use_other(2, 4, 0, 4)
     give_back(2)
+    give_back(3)
     rhs_ref[...] = finish(
         sum_own[...].astype(jnp.bfloat16).astype(jnp.float32), mine, z, inner_i
     )
-    take_sparse(3)
-    use_other(3, (0, 4))
-    give_back(3)
 
     give_energies.wait_recv()
     for part in range(len(cuts) - 1):

time: 139 us -> 87.4 us (0.63)
  Pallas kernels: 133 us -> 81.1 us
    pallas_call x1, Pallas kernels: 133 us -> 81.1 us  [split_both(): pl.pallas_call(functools.partial(block_kernel, cuts, chunks), out_shape=(...]
where the time goes in v3:
time: 87.4 us; the launch traced here: 87.2 us
  Pallas kernels  81.1 us (93%)
  local copies, waits for them, and re-layouts  4.83 us (6%)
    pallas_call x1, Pallas kernels, split_both(): pl.pallas_call(functools.partial(block_kernel, cuts, chunks), out_shape=(...  81.1 us
    unnamed x8, local copies, waits for them, and re-layouts  3.96 us

profile of v3, /device:TPU:0, one launch (start us, length us, event | category | flops | bytes accessed | tf_op | source)
XLA Modules:
  0.0 87.2 jit_solution(852106018523757046)
XLA Ops:
  0.6 0.0 copy-start
  0.6 1.4 %copy-done = bf16[800,1024]{1,0:T(8,128)(2,1)S(1)} copy-done((bf16[800,1024]{1,0:T(8,128)(2,1)S(1)}, bf16[800,1024]{1,0:T(8,128)(2,1)}, u32[]{:S(2)}) %copy-start) | copy-done | bytes 1638424
  2.1 0.0 copy-start.1
  2.1 1.2 %copy-done.1 = bf16[512,1024]{1,0:T(8,128)(2,1)S(1)} copy-done((bf16[512,1024]{1,0:T(8,128)(2,1)S(1)}, bf16[512,1024]{1,0:T(8,128)(2,1)}, u32[]{:S(2)}) %copy-start.1) | copy-done | bytes 1048600
  3.3 0.0 copy-start.2
  3.3 0.7 copy-done.2
  3.9 0.0 copy-start.3
  3.9 0.7 copy-done.3
  4.6 81.1 %shard_map.59 = (bf16[16,12,800]{2,1,0:T(8,128)(2,1)S(1)}, f32[1,800]{1,0:T(1,128)S(1)}) custom-call(bf16[512,1024]{1,0:T(8,128)(2,1)S(1)} %copy-done.1, bf16[800,1024]{1,0:T(8,128)(2,1)S(1)} %copy-done, s32[1,12]{1,0:T(1,128)S(1)} %copy-done.2, f32[1,12]{1,0:T(1,128)S(1)} %bitcast.1), custom_call_target="tpu_custom_call" | custom-call | flops 13421772800 | bytes 2686976 | tf_op jit(solution)/shard_map/pallas_call | solution.py:404
  85.7 0.9 %reshape.14 = bf16[192,800]{1,0:T(8,128)(2,1)} reshape(bf16[16,12,800]{2,1,0:T(8,128)(2,1)S(1)} %get-tuple-element.4) | data formatting | bytes 614400 | tf_op jit(solution)/shard_map/reshape | solution.py:452
  86.6 0.6 reduce
Async XLA Ops:
  0.6 1.4 %copy-start = (bf16[800,1024]{1,0:T(8,128)(2,1)S(1)}, bf16[800,1024]{1,0:T(8,128)(2,1)}, u32[]{:S(2)}) copy-start(bf16[800,1024]{1,0:T(8,128)(2,1)} %s_hbm.1) | copy-start | bytes 4915204
  2.1 1.2 %copy-start.1 = (bf16[512,1024]{1,0:T(8,128)(2,1)S(1)}, bf16[512,1024]{1,0:T(8,128)(2,1)}, u32[]{:S(2)}) copy-start(bf16[512,1024]{1,0:T(8,128)(2,1)} %a_hbm.1) | copy-start | bytes 3145732
  3.3 0.7 copy-start.2
  3.9 0.7 copy-start.3

commit v4 on v3

--- a/solution.py
+++ b/solution.py
@@ -9,7 +9,7 @@
 
 EPS = 1e-06
 LANES = 128
-VMEM_BUDGET = 44 * 1024 * 1024
+VMEM_BUDGET = 60 * 1024 * 1024
 
 
 def inverse_norms(values):
@@ -62,6 +62,8 @@
     META = chunks
     items = [0, META] + list(range(1, chunks))
     last = chunks - 1
+    ahead = chunks // 2
+    quarter = chunks // 4
 
     me = lax.axis_index("env")
     core = me % 2
@@ -105,6 +107,10 @@
     def hand(src, dst, item, send, device):
         return remote(piece(src, item), piece(dst, item), send.at[item], recv.at[dst, item], device)
 
+    def hand_own(dst, item, send, device):
+        here = metas.at[own] if item == META else a_hbm.at[pl.ds(item * rows, rows)]
+        return remote(here, piece(dst, item), send.at[item], recv.at[dst, item], device)
+
     def to_side(q, item):
         return hand(q, 4 + q, item, send_side.at[q], side)
 
@@ -112,7 +118,7 @@
         return hand(q, q + 1, item, send_y.at[q // 2], over)
 
     def to_part(item):
-        return hand(own, 8 - 6 * inner_i, item, send_part, partner)
+        return hand_own(8 - 6 * inner_i, item, send_part, partner)
 
     def to_cross(src, dst, item):
         return hand(src, dst, item, send_cross.at[dst // 2], cross)
@@ -150,18 +156,19 @@
 
         @pl.when(inner)
         def _():
-            to_cross(own, 0, item).start()
+            hand_own(0, item, send_cross.at[0], cross).start()
 
         @pl.when(outer)
         def _():
-            to_over(0, item).start()
-            to_side(0, item).start()
+            hand_own(1, item, send_y.at[0], over).start()
+            hand_own(4, item, send_side.at[0], side).start()
 
     pl.semaphore_wait(barrier, 3 + inner_i)
-    local[0].wait()
-    send_own(0)
-
-    for copy in local[1:]:
+    give_sparse(0).start()
+    for item in range(ahead - 1):
+        send_own(item)
+
+    for copy in local:
         copy.wait()
     ones = jnp.ones((8, depth), jnp.bfloat16)
     contract = (((1,), (1,)), ((), ()))
@@ -191,7 +198,7 @@
     metas[own, 2:3, 0:LANES] = spread(counts_f, down <= along)
     metas[own, 3:4, 0:LANES] = spread(energies_ref[...], down == along)
     send_own(META)
-    send_own(1)
+    send_own(ahead - 1)
 
     def scale_rows(points, inv, start, stop):
         values = points[start:stop, :].astype(jnp.float32)
@@ -254,11 +261,14 @@
         for item in items_of(j):
             @pl.when(inner)
             def _():
+                arrived(8, item)
                 to_cross(8, 2, item).start()
 
             @pl.when(outer)
             def _():
+                arrived(2, item)
                 to_over(2, item).start()
+                to_side(2, item).start()
 
     def pass_aside(q, j):
         for item in items_of(j):
@@ -276,18 +286,13 @@
                 arrived(0, item)
                 to_over(0, item).start()
                 to_side(0, item).start()
-                arrived(8, item)
-
-            @pl.when(outer)
-            def _():
-                arrived(2, item)
-                to_side(2, item).start()
-
-        if j + 2 < chunks:
-            send_own(j + 2)
+
+        if j + ahead < chunks:
+            send_own(j + ahead)
         else:
-            second_wave(j + 2 - chunks)
-            give_sparse(j + 2 - chunks).start()
+            second_wave(j + ahead - chunks)
+        if j == 3 * quarter:
+            give_sparse(1).start()
         if j > 0:
             pass_aside(1, j - 1)
 
@@ -303,10 +308,12 @@
                 to_over(2, item).start()
                 to_side(2, item).start()
 
-        if j + 2 < chunks:
-            second_wave(j + 2)
-        else:
-            give_sparse(j).start()
+        if j + ahead < chunks:
+            second_wave(j + ahead)
+        if j == quarter:
+            give_sparse(2).start()
+        if j == 2 * quarter:
+            give_sparse(3).start()
         if j == 0:
             pass_aside(1, last)
             for i in range(chunks):
@@ -314,20 +321,20 @@
             use_own(1, 1)
         else:
             pass_aside(3, j - 1)
-        if j == 1:
+        if j == chunks // 2 - 1:
             take_sparse(0)
             use_other(0, 1, 0, 2)
-        if j == 2:
-            for i in range(2):
+        if j == 3 * quarter - 1:
+            for i in range(chunks // 2):
                 aside(2, i)
             use_own(2, 1, 0, half)
-    for j in range(2, chunks):
+    for j in range(chunks // 2, chunks):
         aside(2, j)
     use_own(2, 1, half)
-    use_other(0, 1, 2, 1)
+    take_sparse(1)
+    use_other(1, 2, 0, 2)
     pass_aside(3, last)
-    take_sparse(1)
-    use_other(1, 2, 0, 3)
+    use_other(0, 2, 2, 1)
     for j in range(chunks):
         aside(3, j)
     use_own(3, 1)
@@ -386,7 +393,7 @@
 
         @pl.when(inner)
         def _():
-            to_cross(own, 0, item).wait_send()
+            hand_own(0, item, send_cross.at[0], cross).wait_send()
             to_cross(8, 2, item).wait_send()
 
 

time: 87.4 us -> 85.1 us (0.974)
  local copies, waits for them, and re-layouts: 4.83 us -> 1.89 us
    unnamed x8 -> x0, local copies, waits for them, and re-layouts: 3.96 us -> none
    reshape x1, local copies, waits for them, and re-layouts: 0.87 us -> 1.89 us  [split_both(): return (design.reshape(n_env * n_conf, n_sparse), rhs.reshape(n_sparse))]
where the time goes in v4:
time: 85.1 us; the launch traced here: 85 us
  Pallas kernels  81.2 us (95%)
  local copies, waits for them, and re-layouts  1.89 us (2%)
  other arithmetic  1.28 us (2%)
    pallas_call x1, Pallas kernels, split_both(): pl.pallas_call(functools.partial(block_kernel, cuts, chunks), out_shape=(...  81.2 us
    reshape x1, local copies, waits for them, and re-layouts, split_both(): return (design.reshape(n_env * n_conf, n_sparse), rhs.reshape(n_sparse))  1.89 us

profile of v4, /device:TPU:0, one launch (start us, length us, event | category | flops | bytes accessed | tf_op | source)
XLA Modules:
  0.0 85.0 jit_solution(17855154565536138078)
XLA Ops:
  0.6 81.2 %shard_map.59 = (bf16[16,12,800]{2,1,0:T(8,128)(2,1)}, f32[1,800]{1,0:T(1,128)}) custom-call(bf16[512,1024]{1,0:T(8,128)(2,1)} %a_hbm.1, bf16[800,1024]{1,0:T(8,128)(2,1)} %s_hbm.1, s32[1,12]{1,0:T(1,128)} %counts_hbm.1, f32[1,12]{1,0:T(1,128)} %bitcast.1), custom_call_target="tpu_custom_call" | custom-call | flops 13421772800 | bytes 2686976 | tf_op jit(solution)/shard_map/pallas_call | solution.py:411
  81.8 1.9 %reshape.14 = bf16[192,800]{1,0:T(8,128)(2,1)} reshape(bf16[16,12,800]{2,1,0:T(8,128)(2,1)} %get-tuple-element.4) | data formatting | bytes 614400 | tf_op jit(solution)/shard_map/reshape | solution.py:459
  83.7 1.3 %reduce = f32[800]{0:T(1024)} reduce(f32[1,800]{1,0:T(1,128)} %get-tuple-element.5, f32[]{:T(128)} %constant.2), dimensions={0}, to_apply=%get-tuple-element.5.reduce_sub_computation | reduce | bytes 6404 | tf_op jit(solution)/shard_map/pallas_call | solution.py:411
